TPU v7x, 32 devices: a whole 2x2x4 slice. The times are simulated.
32 devices in a mesh: groups: 2 (over x), ctx: 16 (over z, y, core).
Axes of the slice: x: 2, y: 2, z: 4, core: 2. Of those that a mesh axis runs over, the one named last changes fastest.
Arguments:
- events: bfloat16 [16384, 1024], P(('groups', 'ctx')), parts along dimension 0, may hold values from -6 to 6
- w_in: bfloat16 [1024, 4096], replicated, may hold values from -0.1875 to 0.1875
- w_out: bfloat16 [1024, 1024], replicated, may hold values from -0.1875 to 0.1875
- rel_bias: float32 [16, 16], replicated, may hold values from -3 to 3
- lengths: int32 [8], P('groups'), parts along dimension 0, may hold values from 1 to 4096, as said below
- block_lists: int32 [32, 2], P(('groups', 'ctx')), parts along dimension 0, may hold values from 1 to 4, as said below
- candidates: int32 [32, 128], P('groups'), parts along dimension 0, may hold values from 0 to 8191, as said below
Outputs:
- layer_output: bfloat16 [16384, 1024], P(('groups', 'ctx')), parts along dimension 0
- next_score: float32 [16384], P(('groups', 'ctx')), parts along dimension 0
- candidate_score_table: float32 [16384, 128], P(('groups', 'ctx')), parts along dimension 0
There are 2 independent parts, one for each index of `groups`. A program takes and returns all parts, laid end to end along the dimension named above; an argument that names none is the same for every part. Nothing has to cross between parts.
Inputs may be any that keep to these rules, and one draw needn't show every extreme that they name: `lengths`: the first user has exactly 4096 events. `block_lists`: each row holds 2 different distances; row 0 lists distance 1. `candidates`: of one row's 128 rows at most 16 lie in one block, and exactly 16 in some block.
All inputs are finite; a program needn't handle non-finite values.
Results may differ from a plain program's by a relative error of at most 0.007.
Values may be sent and summed in bfloat16 or wider, within the bound.
A program may use at most 128 MiB of HBM per device.

v0:
```python
import jax
import jax.numpy as jnp
from jax import lax
from jax.experimental import pallas as pl
from jax.experimental.pallas import tpu as pltpu
from jax.sharding import PartitionSpec as P

SPAN = 4
NEG = -1e30
TILE = 128
PAIR = 128
VMEM_LIMIT = 56 * 1024 * 1024
BUFFER_OF = ((6, 5, 4, 3), (0, 5, 6, 3), (2, 1, 4, 3), (0, 1, 2, 3))
NBUF = 7

NT = (((1,), (1,)), ((), ()))


def user_of(positions, user_ends):
    return jnp.sum((positions[:, None] >= user_ends[None, :]).astype(jnp.int32), axis=1)


def half_silu(u):
    return u * jnp.tanh(u) + u


def normalize(x):
    center = x - jnp.mean(x, -1, keepdims=True)
    spread = jnp.mean(center * center, -1, keepdims=True)
    return center * lax.rsqrt(spread + 1e-05)


def bucket_of(distance, buckets):
    return min(int(distance).bit_length(), buckets - 1) if distance > 0 else 0


def bias_tile(rel_ref, head, step, buckets):
    if step < 0:
        return jnp.full((TILE, TILE), NEG, jnp.float32)
    row = lax.broadcasted_iota(jnp.int32, (TILE, TILE), 0)
    col = lax.broadcasted_iota(jnp.int32, (TILE, TILE), 1)
    diff = row - col
    first = bucket_of(step * TILE - TILE + 1, buckets)
    last = bucket_of(step * TILE + TILE - 1, buckets)
    value = jnp.full((TILE, TILE), rel_ref[head, first] * 0.5, jnp.float32)
    for b in range(first + 1, last + 1):
        value = jnp.where(diff >= 2 ** (b - 1) - step * TILE, rel_ref[head, b] * 0.5, value)
    if step == 0:
        value = jnp.where(diff >= 0, value, NEG)
    return value


def fill_slab(slab, index, rel_ref, head, top, width, buckets):
    for step in range(top - width + 1, top + 2):
        tile = bias_tile(rel_ref, head, step, buckets)
        for a in range(2):
            p = top + a - step
            if 0 <= p < width:
                slab[index, a * TILE : (a + 1) * TILE, p * TILE : (p + 1) * TILE] = tile


def pair_operands(q, k, v, qm, hot):
    low = lax.broadcasted_iota(jnp.int32, (1, PAIR), 1) < PAIR // 2
    zero = jnp.zeros((), jnp.bfloat16)
    for side in range(2):
        mine = low if side == 0 else jnp.logical_not(low)
        yield (
            jnp.where(mine, q, qm),
            jnp.where(mine, k, hot),
            jnp.where(mine, v, zero),
        )


def first_kernel(
    x_ref, w_hbm, rel_ref, qm_ref, hot_ref, gate_ref, q_ref, att_ref, w, normed, k_ref, v_ref, slab, sems
):
    rows, width = x_ref.shape
    heads, buckets = rel_ref.shape
    order = (1, 3, 2, 0)
    copies = {
        g: pltpu.make_async_copy(
            w_hbm.at[:, g * width : (g + 1) * width], w.at[g], sems.at[g]
        )
        for g in order
    }
    for g in order:
        copies[g].start()
    normed[...] = normalize(x_ref[...].astype(jnp.float32)).astype(jnp.bfloat16)

    def project(g, out, scale):
        def step(j, carry):
            cols = pl.ds(pl.multiple_of(j * 256, 256), 256)
            u = 0.5 * jnp.dot(normed[...], w[g, :, cols], preferred_element_type=jnp.float32)
            y = half_silu(u).astype(jnp.bfloat16)
            out[:, cols] = y if scale is None else y * jnp.asarray(scale, jnp.bfloat16)
            return carry

        copies[g].wait()
        lax.fori_loop(0, width // 256, step, 0)

    project(1, q_ref, 0.5 * (width // heads) ** -0.5)
    project(3, k_ref, None)
    project(2, v_ref, None)
    project(0, gate_ref, None)

    half = rows // 2

    def pair(hp, carry):
        cols = pl.ds(pl.multiple_of(hp * PAIR, PAIR), PAIR)
        for side in range(2):
            fill_slab(slab, side, rel_ref, 2 * hp + side, 2, 4, buckets)
        tops = []
        for side, (q, k, v) in enumerate(
            pair_operands(q_ref[:, cols], k_ref[:, cols], v_ref[:, cols], qm_ref[...], hot_ref[...])
        ):
            s0 = lax.dot_general(q[:half], k[:half], NT, preferred_element_type=jnp.float32)
            s1 = lax.dot_general(q[half:], k, NT, preferred_element_type=jnp.float32)
            w0 = half_silu(s0 + slab[side, :, half:]).astype(jnp.bfloat16)
            w1 = half_silu(s1 + slab[side]).astype(jnp.bfloat16)
            tops.append(
                (
                    jnp.dot(w0, v[:half], preferred_element_type=jnp.float32),
                    jnp.dot(w1, v, preferred_element_type=jnp.float32),
                )
            )
        att_ref[:half, cols] = tops[0][0] + tops[1][0]
        att_ref[half:, cols] = tops[0][1] + tops[1][1]
        return carry

    lax.fori_loop(0, heads // 2, pair, 0)


def second_kernel(
    info_ref, rel_ref, x_ref, gate_ref, q_ref, own_ref, qm_ref, hot_ref, cand_ref, follow_ref, ok_ref,
    w_hbm, wout_hbm, *rest
):
    bufs = rest[:NBUF]
    out_ref, next_ref, table_ref = rest[NBUF : NBUF + 3]
    picked, wkv, wout, normed, kv, att, slab, sems = rest[NBUF + 3 :]
    rows, width = x_ref.shape
    heads, buckets = rel_ref.shape
    picks = hot_ref.shape[0]
    half = rows // 2
    for p in range(picks):
        for n in range(NBUF):
            @pl.when(info_ref[p, 0] == n)
            def _():
                pltpu.make_async_copy(bufs[n], picked.at[p], sems.at[p]).start()
    w_copy = pltpu.make_async_copy(w_hbm.at[:, 2 * width :], wkv, sems.at[picks])
    o_copy = pltpu.make_async_copy(wout_hbm, wout, sems.at[picks + 1])
    w_copy.start()
    o_copy.start()
    att[...] = own_ref[...]
    for p in range(picks):
        pltpu.make_async_copy(bufs[0], picked.at[p], sems.at[p]).wait()
    w_copy.wait()
    for p in range(picks):
        @pl.when(info_ref[p, 2] == 1)
        def _(p=p):
            distance = info_ref[p, 1]
            normed[...] = normalize(picked[p].astype(jnp.float32)).astype(jnp.bfloat16)

            def step(j, carry):
                cols = pl.ds(pl.multiple_of(j * 256, 256), 256)
                u = 0.5 * jnp.dot(normed[...], wkv[:, cols], preferred_element_type=jnp.float32)
                kv[:, cols] = half_silu(u).astype(jnp.bfloat16)
                return carry

            lax.fori_loop(0, 2 * width // 256, step, 0)
            for d in range(1, SPAN + 1):
                @pl.when(distance == d)
                def _(d=d):
                    def fill(h, carry):
                        fill_slab(slab, h, rel_ref, h, (rows // TILE) * d + 2, 6, buckets)
                        return carry

                    lax.fori_loop(0, heads, fill, 0)

            def pair(hp, carry):
                cols = pl.ds(pl.multiple_of(hp * PAIR, PAIR), PAIR)
                kcols = pl.ds(pl.multiple_of(width + hp * PAIR, PAIR), PAIR)
                tops = []
                for side, (q, k, v) in enumerate(
                    pair_operands(q_ref[:, cols], kv[:, kcols], kv[:, cols], qm_ref[...], hot_ref[p])
                ):
                    h = 2 * hp + side
                    s0 = lax.dot_general(q[:half], k, NT, preferred_element_type=jnp.float32)
                    s1 = lax.dot_general(q[half:], k, NT, preferred_element_type=jnp.float32)
                    w0 = half_silu(s0 + slab[h, :, half:]).astype(jnp.bfloat16)
                    w1 = half_silu(s1 + slab[h, :, :rows]).astype(jnp.bfloat16)
                    tops.append(
                        (
                            jnp.dot(w0, v, preferred_element_type=jnp.float32),
                            jnp.dot(w1, v, preferred_element_type=jnp.float32),
                        )
                    )
                att[:half, cols] += tops[0][0] + tops[1][0]
                att[half:, cols] += tops[0][1] + tops[1][1]
                return carry

            lax.fori_loop(0, heads // 2, pair, 0)
    o_copy.wait()
    scale = width**-0.5

    def finish(r, carry):
        rs = pl.ds(pl.multiple_of(r * 256, 256), 256)
        gated = (normalize(att[rs, :]) * gate_ref[rs, :].astype(jnp.float32)).astype(jnp.bfloat16)
        added = jnp.dot(gated, wout[...], preferred_element_type=jnp.float32)
        layer = (x_ref[rs, :].astype(jnp.float32) + added).astype(jnp.bfloat16)
        out_ref[rs, :] = layer
        inner = jnp.sum(
            layer.astype(jnp.float32) * follow_ref[rs, :].astype(jnp.float32), axis=1, keepdims=True
        )
        next_ref[rs, :] = jnp.where(ok_ref[rs, :] > 0, inner * scale, 0.0)
        table_ref[rs, :] = (
            lax.dot_general(layer, cand_ref[...], NT, preferred_element_type=jnp.float32) * scale
        )
        return carry

    lax.fori_loop(0, rows // 256, finish, 0)


def slot_ids(request, ctx_size, event_row_count, slot_cap):
    owner_dev = request // event_row_count
    local_row = request % event_row_count
    owner_hits = (owner_dev[:, None] == jnp.arange(ctx_size, dtype=jnp.int32)[None, :]).astype(
        jnp.int32
    )
    slot_rank = jnp.sum(jnp.cumsum(owner_hits, axis=0) * owner_hits, axis=1) - 1
    slot_id = owner_dev * slot_cap + slot_rank
    slot_hits = slot_id[:, None] == jnp.arange(ctx_size * slot_cap, dtype=jnp.int32)[None, :]
    row_ids = jnp.sum(jnp.where(slot_hits, local_row[:, None] + 1, 0), axis=0) - 1
    return (row_ids.reshape(ctx_size, slot_cap), slot_hits)


def received(events, count):
    planes = count // SPAN
    shift = planes // 4

    def flows(plane):
        later = (plane + shift) % planes + 1
        return later < planes and later != planes // 2

    def inside(moves, wanted=None):
        return [
            (p * SPAN + s, p * SPAN + t)
            for p in range(planes)
            if wanted is None or wanted(p)
            for s, t in moves
        ]

    def fed(plane):
        return flows((plane - 1) % planes)

    across = [
        (p * SPAN + l, (p * SPAN + l + SPAN) % count)
        for p in range(planes)
        if flows(p)
        for l in range(SPAN)
    ]
    b1 = lax.ppermute(events, "ctx", across)
    a2 = lax.ppermute(events, "ctx", inside(((0, 2), (1, 3))))
    a1 = lax.ppermute(events, "ctx", inside(((0, 1), (2, 3))))
    b3 = lax.ppermute(b1, "ctx", inside(((2, 0), (3, 1)), fed))
    b2 = lax.ppermute(b1, "ctx", inside(((1, 0), (3, 2)), fed))
    a3 = lax.ppermute(a2, "ctx", inside(((2, 3), (3, 2))))
    b4 = lax.ppermute(b3, "ctx", inside(((0, 1), (1, 0)), fed))
    return (a1, a2, a3, b1, b2, b3, b4)


def fetch_candidates(events, candidates, ctx_size, my_index):
    event_row_count, hidden_width = events.shape
    cand_count = candidates.shape[1]
    slot_cap = 2 * cand_count // ctx_size
    own_request = lax.dynamic_slice_in_dim(candidates, my_index, 1, 0)[0]
    own_hits = slot_ids(own_request, ctx_size, event_row_count, slot_cap)[1]
    every_ids = jax.vmap(lambda request: slot_ids(request, ctx_size, event_row_count, slot_cap)[0])(
        candidates
    )
    my_part = lax.dynamic_index_in_dim(every_ids, my_index, 1, keepdims=False)
    flat_ids = my_part.reshape(-1)
    picks = (flat_ids[:, None] == jnp.arange(event_row_count, dtype=jnp.int32)[None, :]).astype(
        jnp.bfloat16
    )
    fetched = jnp.dot(picks, events, preferred_element_type=jnp.float32).astype(jnp.bfloat16)
    arrived_rows = lax.all_to_all(
        fetched.reshape(my_part.shape + (hidden_width,)), "ctx", split_axis=0, concat_axis=0, tiled=True
    )
    flat_rows = arrived_rows.reshape(ctx_size * slot_cap, hidden_width)
    return jnp.dot(
        own_hits.astype(jnp.bfloat16), flat_rows, preferred_element_type=jnp.float32
    ).astype(jnp.bfloat16)


def shards(events, w_in, w_out, rel_bias, lengths, block_lists, candidates):
    rows, width = events.shape
    heads = rel_bias.shape[0]
    users = lengths.shape[0]
    picks = block_lists.shape[1]
    count = lax.axis_size("ctx")
    my_index = lax.axis_index("ctx")
    total_rows = count * rows
    user_ends = jnp.cumsum(lengths)

    def times_of(block_num):
        return (
            block_num * rows + jnp.arange(rows, dtype=jnp.int32) + total_rows // 4
        ) % total_rows

    query_pos = times_of(my_index)
    query_user = user_of(query_pos, user_ends)
    lane = jnp.arange(PAIR, dtype=jnp.int32)[None, :] % (PAIR // 2)
    qm = jnp.where((lane == query_user[:, None]) | (lane > users), 0.0, NEG).astype(jnp.bfloat16)
    own_hot = (lane == query_user[:, None]).astype(jnp.bfloat16)

    table = jnp.asarray(BUFFER_OF, jnp.int32)[my_index % SPAN]
    infos, hots = [], []
    for p in range(picks):
        distance = block_lists[0, p]
        key_pos = times_of((my_index - distance) % count)
        key_user = user_of(key_pos, user_ends)
        useful = (key_pos[0] < query_pos[0]) & (key_user[rows - 1] >= query_user[0])
        infos.append(jnp.stack([table[distance - 1], distance, useful.astype(jnp.int32)]))
        hots.append((lane == key_user[:, None]).astype(jnp.bfloat16))
    info = jnp.stack(infos)
    hot = jnp.stack(hots)

    bufs = received(events, count)
    next_first = lax.ppermute(
        events[:1], "ctx", [((s + 1) % count, s) for s in range(count)]
    )
    following = jnp.concatenate([events[1:], next_first], axis=0)
    next_ok = (user_of(query_pos + 1, user_ends) == query_user) & (query_pos + 1 < total_rows)
    cand = fetch_candidates(events, candidates, count, my_index)

    vm = pl.BlockSpec(memory_space=pltpu.VMEM)
    sm = pl.BlockSpec(memory_space=pltpu.SMEM)
    hb = pl.BlockSpec(memory_space=pl.ANY)
    bf, f32 = jnp.bfloat16, jnp.float32
    gate, q, own = pl.pallas_call(
        first_kernel,
        out_shape=(
            jax.ShapeDtypeStruct((rows, width), bf),
            jax.ShapeDtypeStruct((rows, width), bf),
            jax.ShapeDtypeStruct((rows, width), f32),
        ),
        in_specs=[vm, hb, sm, vm, vm],
        out_specs=(vm, vm, vm),
        scratch_shapes=[
            pltpu.VMEM((4, width, width), bf),
            pltpu.VMEM((rows, width), bf),
            pltpu.VMEM((rows, width), bf),
            pltpu.VMEM((rows, width), bf),
            pltpu.VMEM((2, 2 * TILE, 4 * TILE), f32),
            pltpu.SemaphoreType.DMA((4,)),
        ],
        compiler_params=pltpu.CompilerParams(vmem_limit_bytes=VMEM_LIMIT),
        cost_estimate=pl.CostEstimate(
            flops=2 * rows * width * 4 * width + 4 * rows * rows * width,
            bytes_accessed=10 * width * width,
            transcendentals=heads * rows * rows,
        ),
        name="project_and_own_block",
    )(events, w_in, rel_bias, qm, own_hot)
    layer_output, next_score, scores = pl.pallas_call(
        second_kernel,
        out_shape=(
            jax.ShapeDtypeStruct((rows, width), bf),
            jax.ShapeDtypeStruct((rows, 1), f32),
            jax.ShapeDtypeStruct((rows, candidates.shape[1]), f32),
        ),
        in_specs=[sm, sm, vm, vm, vm, vm, vm, vm, vm, vm, vm, hb, hb] + [hb] * NBUF,
        out_specs=(vm, vm, vm),
        scratch_shapes=[
            pltpu.VMEM((picks, rows, width), bf),
            pltpu.VMEM((width, 2 * width), bf),
            pltpu.VMEM((width, width), bf),
            pltpu.VMEM((rows, width), bf),
            pltpu.VMEM((rows, 2 * width), bf),
            pltpu.VMEM((rows, width), f32),
            pltpu.VMEM((heads, 2 * TILE, 6 * TILE), f32),
            pltpu.SemaphoreType.DMA((picks + 2,)),
        ],
        compiler_params=pltpu.CompilerParams(vmem_limit_bytes=VMEM_LIMIT),
        cost_estimate=pl.CostEstimate(
            flops=2 * picks * (2 * rows * width * width + 2 * rows * rows * width),
            bytes_accessed=16 * width * width,
            transcendentals=2 * heads * rows * rows,
        ),
        name="earlier_blocks_and_output",
    )(
        info, rel_bias, events, gate, q, own, qm, hot, cand, following,
        next_ok.astype(f32)[:, None], w_in, w_out, *bufs,
    )
    return (layer_output, next_score[:, 0], scores)


def solution(mesh):
    in_specs = (
        P(("groups", "ctx"), None),
        P(),
        P(),
        P(),
        P("groups"),
        P(("groups", "ctx"), None),
        P("groups", None),
    )
    out_specs = (P(("groups", "ctx"), None), P(("groups", "ctx")), P(("groups", "ctx"), None))
    return jax.shard_map(shards, mesh=mesh, in_specs=in_specs, out_specs=out_specs, check_vma=False)
```

profile of v0, /device:TPU:0, one launch (start us, length us, event | category | flops | bytes accessed | tf_op | source)
XLA Modules:
  0.0 124.6 jit_solution(2210303990394652455)
XLA Ops:
  0.6 0.0 copy-start.3
  0.6 0.0 copy-start.2
  0.7 0.0 copy-start.4
  0.7 5.1 %collective-permute-start.2 = (bf16[512,1024]{1,0:T(8,128)(2,1)}, bf16[512,1024]{1,0:T(8,128)(2,1)S(1)}, u32[]{:S(2)}, u32[]{:S(2)}) collective-permute-start(bf16[512,1024]{1,0:T(8,128)(2,1)} %x_ref.3), channel_id=1, source_target_pairs={{0,2},{1,3},{4,6},{5,7},{8,10},{9,11},{12,14},{13,15},{16,18},{17,... | collective-permute-start | bytes 3145736 | tf_op jit(solution)/shard_map/ppermute | solution.py:262
  5.7 2.5 %collective-permute-start.1 = (bf16[512,1024]{1,0:T(8,128)(2,1)}, bf16[512,1024]{1,0:T(8,128)(2,1)}, u32[]{:S(2)}, u32[]{:S(2)}) collective-permute-start(bf16[512,1024]{1,0:T(8,128)(2,1)} %x_ref.3), channel_id=1, source_target_pairs={{0,1},{2,3},{4,5},{6,7},{8,9},{10,11},{12,13},{14,15},{16,17},{18,... | collective-permute-start | bytes 3145736 | tf_op jit(solution)/shard_map/ppermute | solution.py:263
  8.2 1.3 %collective-permute-start.4 = (bf16[512,1024]{1,0:T(8,128)(2,1)}, bf16[512,1024]{1,0:T(8,128)(2,1)}, u32[]{:S(2)}, u32[]{:S(2)}) collective-permute-start(bf16[512,1024]{1,0:T(8,128)(2,1)} %x_ref.3), channel_id=1, source_target_pairs={{4,8},{5,9},{6,10},{7,11},{12,0},{13,1},{14,2},{15,3},{20,24},{21,... | collective-permute-start | bytes 3145736 | tf_op jit(solution)/shard_map/ppermute | solution.py:261
  9.5 0.7 slice.41
  10.2 2.2 %collective-permute-start = (bf16[1,1024]{1,0:T(2,128)(2,1)S(1)}, bf16[1,1024]{1,0:T(2,128)(2,1)S(1)}, u32[]{:S(2)}, u32[]{:S(2)}) collective-permute-start(bf16[1,1024]{1,0:T(2,128)(2,1)S(1)} %slice.41), channel_id=1, source_target_pairs={{1,0},{2,1},{3,2},{4,3},{5,4},{6,5},{7,6},{8,7},{9,8},{10,9},{11,1... | collective-permute-start | bytes 6152 | tf_op jit(solution)/shard_map/ppermute | solution.py:329
  12.4 0.7 add_select_fusion.2
  13.1 0.1 copy.28
  13.2 2.8 %select_reduce_fusion.1 = s32[16,128]{0,1:T(8,128)S(1)} fusion(s32[16,128]{0,1:T(8,128)S(1)} %copy.28), kind=kOutput, calls=%fused_computation.5 | output fusion | flops 4323328 | bytes 16384 | tf_op jit(solution)/shard_map/vmap(jit(cumsum))/reduce_window_sum | solution.py:229
  16.0 0.1 copy.29
  16.1 0.7 add_add_fusion
  16.8 0.7 select_reduce_fusion
  17.5 0.1 sub.47
  17.7 0.1 eq.172
  17.7 2.5 %convolution_convert_fusion = bf16[256,1024]{1,0:T(8,128)(2,1)} fusion(bf16[512,1024]{1,0:T(8,128)(2,1)} %x_ref.3, s32[256]{0:T(256)S(1)} %eq.172), kind=kOutput, calls=%fused_computation.2 | convolution fusion | flops 268828672 | bytes 1573888 | tf_op jit(solution)/shard_map/dot_general | solution.py:285
  20.2 4.7 %all-to-all-start = ((bf16[16,16,1024]{2,1,0:T(8,128)(2,1)}), bf16[16,16,1024]{2,1,0:T(8,128)(2,1)S(1)}, u32[]{:S(2)}, u32[]{:S(2)}) async-start(bf16[16,16,1024]{2,1,0:T(8,128)(2,1)} %bitcast.11), calls=%async_computation | async-start | bytes 1048576 | tf_op jit(solution)/shard_map/all_to_all | solution.py:286
  25.0 0.0 copy-done.2
  25.0 0.6 fusion.18
  29.4 0.0 copy-done.4
  29.4 0.2 reduce-window.8
  29.6 0.6 slice.33
  30.2 0.5 slice.34
  30.7 0.1 convert_reduce_fusion
  30.8 0.6 slice.36
  31.4 0.7 slice.35
  34.8 0.7 and_select_fusion
  35.5 0.1 fusion.10
  35.6 0.2 reduce_window_sum.29
  35.7 0.0 copy-done.3
  35.7 0.7 fusion.17
  36.4 0.2 select_reduce_fusion.2
  36.6 0.9 fusion.8.ok_ref
  37.5 0.9 collective-permute-done.4.rest_3_
  38.4 1.3 %collective-permute-start.6 = (bf16[512,1024]{1,0:T(8,128)(2,1)}, bf16[512,1024]{1,0:T(8,128)(2,1)}, u32[]{:S(2)}, u32[]{:S(2)}) collective-permute-start(bf16[512,1024]{1,0:T(8,128)(2,1)} %collective-permute-done.4.rest_3_), channel_id=1, source_target_pairs={{2,0},{3,1},{10,8},{11,9},{18,16},{19,17},{26,24},{27,25}} | collective-permute-start | bytes 3145736 | tf_op jit(solution)/shard_map/ppermute | solution.py:264
  39.7 1.4 %add_bitcast_fusion = s32[1,3]{1,0:T(1,128)S(1)} fusion(s32[1]{0:T(128)S(6)} %convert_element_type.68, s32[1]{0:T(128)} %bitcast.2, s32[1]{0:T(128)} %bitcast.1), kind=kLoop, calls=%fused_computation.66 | loop fusion | flops 6 | bytes 24 | tf_op jit(solution)/shard_map/stack | solution.py:325
  41.0 0.5 slice.38
  42.8 0.6 slice.39
  44.8 0.7 add_add_fusion.1
  45.5 0.8 compare_convert_fusion.hot_ref
  46.3 0.8 select_convert_fusion.qm_ref
  47.1 0.2 broadcast_compare_fusion.1
  47.3 0.8 add_convert_fusion.hot_ref
  48.0 1.3 %collective-permute-start.5 = (bf16[512,1024]{1,0:T(8,128)(2,1)}, bf16[512,1024]{1,0:T(8,128)(2,1)}, u32[]{:S(2)}, u32[]{:S(2)}) collective-permute-start(bf16[512,1024]{1,0:T(8,128)(2,1)} %collective-permute-done.4.rest_3_), channel_id=1, source_target_pairs={{1,0},{3,2},{9,8},{11,10},{17,16},{19,18},{25,24},{27,26}} | collective-permute-start | bytes 3145736 | tf_op jit(solution)/shard_map/ppermute | solution.py:265
  49.3 0.0 collective-permute-done.2.rest_1_
  49.3 0.0 copy-start.1
  49.3 1.7 %collective-permute-start.3 = (bf16[512,1024]{1,0:T(8,128)(2,1)S(1)}, bf16[512,1024]{1,0:T(8,128)(2,1)}, u32[]{:S(2)}, u32[]{:S(2)}) collective-permute-start(bf16[512,1024]{1,0:T(8,128)(2,1)S(1)} %collective-permute-done.2.rest_1_), channel_id=1, source_target_pairs={{2,3},{3,2},{6,7},{7,6},{10,11},{11,10},{14,15},{15,14},{18,19},{1... | collective-permute-start | bytes 3145736 | tf_op jit(solution)/shard_map/ppermute | solution.py:266
  51.0 15.2 %collective-permute-done.6.rest_5_ = bf16[512,1024]{1,0:T(8,128)(2,1)} collective-permute-done((bf16[512,1024]{1,0:T(8,128)(2,1)}, bf16[512,1024]{1,0:T(8,128)(2,1)}, u32[]{:S(2)}, u32[]{:S(2)}) %collective-permute-start.6) | collective-permute-done | bytes 1048608 | tf_op jit(solution)/shard_map/ppermute | solution.py:264
  66.2 1.9 %collective-permute-start.7 = (bf16[512,1024]{1,0:T(8,128)(2,1)}, bf16[512,1024]{1,0:T(8,128)(2,1)}, u32[]{:S(2)}, u32[]{:S(2)}) collective-permute-start(bf16[512,1024]{1,0:T(8,128)(2,1)} %collective-permute-done.6.rest_5_), channel_id=1, source_target_pairs={{0,1},{1,0},{8,9},{9,8},{16,17},{17,16},{24,25},{25,24}} | collective-permute-start | bytes 3145736 | tf_op jit(solution)/shard_map/ppermute | solution.py:267
  68.1 1.3 %add_bitcast_fusion.1 = s32[1,3]{1,0:T(1,128)S(1)} fusion(s32[1]{0:T(128)S(6)} %convert_element_type.70, s32[1]{0:T(128)} %bitcast.8, s32[1]{0:T(128)} %bitcast.7), kind=kLoop, calls=%fused_computation.67 | loop fusion | flops 6 | bytes 24 | tf_op jit(solution)/shard_map/stack | solution.py:325
  69.4 17.8 %project_and_own_block.1 = (bf16[512,1024]{1,0:T(8,128)(2,1)}, bf16[512,1024]{1,0:T(8,128)(2,1)}, f32[512,1024]{1,0:T(8,128)}) custom-call(bf16[512,1024]{1,0:T(8,128)(2,1)} %x_ref.3, bf16[1024,4096]{1,0:T(8,128)(2,1)} %w_hbm.3, f32[16,16]{1,0:T(8,128)} %rel_ref.3, bf16[512,128]{1,0:T(8,128)(2,1)} %select_convert_fusion.qm_ref, ...), custom_call_target="tpu_custom_call" | custom-call | flops 5368709120 | bytes 10485760 | tf_op jit(solution)/shard_map/project_and_own_block/pallas_call | solution.py:340
  87.2 0.6 pad_add_fusion.info_ref
  87.8 0.3 slice.40
  88.0 0.0 collective-permute-done
  88.1 1.1 pad_maximum_fusion.follow_ref
  89.1 0.0 all-to-all-done
  89.1 1.0 convolution_convert_fusion.1.cand_ref
  90.1 0.0 collective-permute-done.1.rest_0_
  90.1 0.0 collective-permute-done.3.rest_2_
  90.1 0.0 collective-permute-done.5.rest_4_
  90.1 0.0 collective-permute-done.7.rest_6_
  90.1 32.8 %earlier_blocks_and_output.1 = (bf16[512,1024]{1,0:T(8,128)(2,1)}, f32[512,1]{1,0:T(8,128)}, f32[512,128]{1,0:T(8,128)}) custom-call(s32[2,3]{1,0:T(2,128)} %pad_add_fusion.info_ref, f32[16,16]{1,0:T(8,128)} %rel_ref.3, bf16[512,1024]{1,0:T(8,128)(2,1)} %x_ref.3, bf16[512,1024]{1,0:T(8,128)(2,1)} %get-tuple-element.9.gate_ref, ...), custom_call_target="tpu_custom_call" | custom-call | flops 6442450944 | bytes 16777216 | tf_op jit(solution)/shard_map/earlier_blocks_and_output/pallas_call | solution.py:365
  122.9 1.7 %reduce.1 = f32[512]{0:T(512)} reduce(f32[512,1]{1,0:T(8,128)} %get-tuple-element.13, f32[]{:T(128)} %constant.178), dimensions={1}, to_apply=%get-tuple-element.13.reduce_sub_computation | reduce | bytes 4100 | tf_op jit(solution)/shard_map/earlier_blocks_and_output/pallas_call | solution.py:365
  (10 shorter events, 0.1 us)
Async XLA Ops:
  0.6 35.1 %copy-start.3 = (s32[4,4]{1,0:T(4,128)S(1)}, s32[4,4]{1,0:T(4,128)}, u32[]{:S(2)}) copy-start(s32[4,4]{1,0:T(4,128)} %constant.175.clone) | copy-start | bytes 196
  0.6 24.3 %copy-start.2 = (s32[1,2]{1,0:T(1,128)S(1)}, s32[1,2]{1,0:T(1,128)}, u32[]{:S(2)}) copy-start(s32[1,2]{1,0:T(1,128)} %param.13) | copy-start | bytes 28
  0.7 28.8 %copy-start.4 = (s32[4]{0:T(128)S(1)}, s32[4]{0:T(128)}, u32[]{:S(2)}) copy-start(s32[4]{0:T(128)} %param.12) | copy-start | bytes 52
  0.7 48.7 %collective-permute-start.2 = (bf16[512,1024]{1,0:T(8,128)(2,1)}, bf16[512,1024]{1,0:T(8,128)(2,1)S(1)}, u32[]{:S(2)}, u32[]{:S(2)}) collective-permute-start(bf16[512,1024]{1,0:T(8,128)(2,1)} %x_ref.3), channel_id=1, source_target_pairs={{0,2},{1,3},{4,6},{5,7},{8,10},{9,11},{12,14},{13,15},{16,18},{17,... | collective-permute-start | bytes 3145736 | tf_op jit(solution)/shard_map/ppermute | solution.py:262
  5.7 84.4 %collective-permute-start.1 = (bf16[512,1024]{1,0:T(8,128)(2,1)}, bf16[512,1024]{1,0:T(8,128)(2,1)}, u32[]{:S(2)}, u32[]{:S(2)}) collective-permute-start(bf16[512,1024]{1,0:T(8,128)(2,1)} %x_ref.3), channel_id=1, source_target_pairs={{0,1},{2,3},{4,5},{6,7},{8,9},{10,11},{12,13},{14,15},{16,17},{18,... | collective-permute-start | bytes 3145736 | tf_op jit(solution)/shard_map/ppermute | solution.py:263
  8.2 30.2 %collective-permute-start.4 = (bf16[512,1024]{1,0:T(8,128)(2,1)}, bf16[512,1024]{1,0:T(8,128)(2,1)}, u32[]{:S(2)}, u32[]{:S(2)}) collective-permute-start(bf16[512,1024]{1,0:T(8,128)(2,1)} %x_ref.3), channel_id=1, source_target_pairs={{4,8},{5,9},{6,10},{7,11},{12,0},{13,1},{14,2},{15,3},{20,24},{21,... | collective-permute-start | bytes 3145736 | tf_op jit(solution)/shard_map/ppermute | solution.py:261
  10.2 77.8 %collective-permute-start = (bf16[1,1024]{1,0:T(2,128)(2,1)S(1)}, bf16[1,1024]{1,0:T(2,128)(2,1)S(1)}, u32[]{:S(2)}, u32[]{:S(2)}) collective-permute-start(bf16[1,1024]{1,0:T(2,128)(2,1)S(1)} %slice.41), channel_id=1, source_target_pairs={{1,0},{2,1},{3,2},{4,3},{5,4},{6,5},{7,6},{8,7},{9,8},{10,9},{11,1... | collective-permute-start | bytes 6152 | tf_op jit(solution)/shard_map/ppermute | solution.py:329
  20.2 68.9 %all-to-all-start = ((bf16[16,16,1024]{2,1,0:T(8,128)(2,1)}), bf16[16,16,1024]{2,1,0:T(8,128)(2,1)S(1)}, u32[]{:S(2)}, u32[]{:S(2)}) async-start(bf16[16,16,1024]{2,1,0:T(8,128)(2,1)} %bitcast.11), calls=%async_computation | async-start | bytes 1048576 | tf_op jit(solution)/shard_map/all_to_all | solution.py:286
  38.4 27.8 %collective-permute-start.6 = (bf16[512,1024]{1,0:T(8,128)(2,1)}, bf16[512,1024]{1,0:T(8,128)(2,1)}, u32[]{:S(2)}, u32[]{:S(2)}) collective-permute-start(bf16[512,1024]{1,0:T(8,128)(2,1)} %collective-permute-done.4.rest_3_), channel_id=1, source_target_pairs={{2,0},{3,1},{10,8},{11,9},{18,16},{19,17},{26,24},{27,25}} | collective-permute-start | bytes 3145736 | tf_op jit(solution)/shard_map/ppermute | solution.py:264
  48.0 42.1 %collective-permute-start.5 = (bf16[512,1024]{1,0:T(8,128)(2,1)}, bf16[512,1024]{1,0:T(8,128)(2,1)}, u32[]{:S(2)}, u32[]{:S(2)}) collective-permute-start(bf16[512,1024]{1,0:T(8,128)(2,1)} %collective-permute-done.4.rest_3_), channel_id=1, source_target_pairs={{1,0},{3,2},{9,8},{11,10},{17,16},{19,18},{25,24},{27,26}} | collective-permute-start | bytes 3145736 | tf_op jit(solution)/shard_map/ppermute | solution.py:265
  49.3 37.9 %copy-start.1 = (bf16[512,1024]{1,0:T(8,128)(2,1)}, bf16[512,1024]{1,0:T(8,128)(2,1)S(1)}, u32[]{:S(2)}) copy-start(bf16[512,1024]{1,0:T(8,128)(2,1)S(1)} %collective-permute-done.2.rest_1_) | copy-start | bytes 3145732
  49.3 40.8 %collective-permute-start.3 = (bf16[512,1024]{1,0:T(8,128)(2,1)S(1)}, bf16[512,1024]{1,0:T(8,128)(2,1)}, u32[]{:S(2)}, u32[]{:S(2)}) collective-permute-start(bf16[512,1024]{1,0:T(8,128)(2,1)S(1)} %collective-permute-done.2.rest_1_), channel_id=1, source_target_pairs={{2,3},{3,2},{6,7},{7,6},{10,11},{11,10},{14,15},{15,14},{18,19},{1... | collective-permute-start | bytes 3145736 | tf_op jit(solution)/shard_map/ppermute | solution.py:266
  66.2 23.9 %collective-permute-start.7 = (bf16[512,1024]{1,0:T(8,128)(2,1)}, bf16[512,1024]{1,0:T(8,128)(2,1)}, u32[]{:S(2)}, u32[]{:S(2)}) collective-permute-start(bf16[512,1024]{1,0:T(8,128)(2,1)} %collective-permute-done.6.rest_5_), channel_id=1, source_target_pairs={{0,1},{1,0},{8,9},{9,8},{16,17},{17,16},{24,25},{25,24}} | collective-permute-start | bytes 3145736 | tf_op jit(solution)/shard_map/ppermute | solution.py:267
  69.4 18.4 %copy-start = (bf16[512,1024]{1,0:T(8,128)(2,1)S(1)}, bf16[512,1024]{1,0:T(8,128)(2,1)}, u32[]{:S(2)}) copy-start(bf16[512,1024]{1,0:T(8,128)(2,1)} %x_ref.3) | copy-start | bytes 3145732
where the time goes:
time: 125 us
  Pallas kernels  50.6 us (40%)
  starting transfers between devices  21.9 us (18%)
  other arithmetic  16.4 us (13%)
  waiting for transfers between devices  16.1 us (13%)
  between operations  10 us (8%)
  local copies, waits for them, and re-layouts  6.07 us (5%)
  matrix products  3.5 us (3%)
    pallas_call x1, Pallas kernels, shards(): pl.pallas_call(second_kernel, out_shape=(jax.ShapeDtypeStruct((rows, widt...  32.8 us
    pallas_call x1, Pallas kernels, shards(): pl.pallas_call(first_kernel, out_shape=(jax.ShapeDtypeStruct((rows, width...  17.8 us
    ppermute x1, waiting for transfers between devices, received(): b3 = lax.ppermute(b1, 'ctx', inside(((2, 0), (3, 1)), fed))  15.2 us
    ppermute x1, starting transfers between devices, received(): a2 = lax.ppermute(events, 'ctx', inside(((0, 2), (1, 3))))  5.07 us
    all_to_all x1, starting transfers between devices, fetch_candidates(): lax.all_to_all(fetched.reshape(my_part.shape + (hidden_width,)), 'ctx', s...  4.72 us
    slice x6, local copies, waits for them, and re-layouts, shards(): useful = (key_pos[0] < query_pos[0]) & (key_user[rows - 1] >= query_user[0])  3.44 us
    another operation x3, other arithmetic, shards(): info = jnp.stack(infos)  3.17 us
    another operation x2, other arithmetic, slot_ids(): slot_rank = jnp.sum(jnp.cumsum(owner_hits, axis=0) * owner_hits, axis=1) - 1  2.96 us
  transfers between devices with their start and end apart: 9, of which 2 were waited for; matrix products, arithmetic and copies ran while one was open for 19% of the time, Pallas kernels for 14%

commit v1 on v0

v1 whole, which is shorter than its diff:
```python
import functools

import jax
import jax.numpy as jnp
from jax import lax
from jax.experimental import pallas as pl
from jax.experimental.pallas import tpu as pltpu
from jax.sharding import PartitionSpec as P

SPAN = 4
NEG = -1e30
TILE = 128
PAIR = 128
VMEM_LIMIT = 56 * 1024 * 1024
CHUNKS = 4
MESH = pl.DeviceIdType.MESH

NT = (((1,), (1,)), ((), ()))


def ends_of(lengths_ref):
    ends, total = [], 0
    for u in range(lengths_ref.shape[0]):
        total = total + lengths_ref[u]
        ends.append(total)
    return ends


def user_of(positions, ends):
    user = jnp.zeros_like(positions)
    for end in ends:
        user = user + (positions >= end).astype(jnp.int32)
    return user


def block_time(block, count):
    return lax.rem(block + count // 4, count)


def user_terms(time, rows, ends):
    row = lax.broadcasted_iota(jnp.int32, (rows, PAIR), 0)
    lane = lax.rem(lax.broadcasted_iota(jnp.int32, (rows, PAIR), 1), PAIR // 2)
    same = lane == user_of(time * rows + row, ends)
    one = jnp.where(same, 1.0, 0.0).astype(jnp.bfloat16)
    other = jnp.where(same, 0.0, NEG).astype(jnp.bfloat16)
    return other, one


def half_silu(u):
    return u * jnp.tanh(u) + u


def normalize(x):
    center = x - jnp.mean(x, -1, keepdims=True)
    spread = jnp.mean(center * center, -1, keepdims=True)
    return center * lax.rsqrt(spread + 1e-05)


def bucket_of(distance, buckets):
    return min(int(distance).bit_length(), buckets - 1) if distance > 0 else 0


def bias_tile(rel_ref, head, step, buckets):
    if step < 0:
        return jnp.full((TILE, TILE), NEG, jnp.float32)
    row = lax.broadcasted_iota(jnp.int32, (TILE, TILE), 0)
    col = lax.broadcasted_iota(jnp.int32, (TILE, TILE), 1)
    diff = row - col
    first = bucket_of(step * TILE - TILE + 1, buckets)
    last = bucket_of(step * TILE + TILE - 1, buckets)
    value = jnp.full((TILE, TILE), rel_ref[head, first] * 0.5, jnp.float32)
    for b in range(first + 1, last + 1):
        value = jnp.where(diff >= 2 ** (b - 1) - step * TILE, rel_ref[head, b] * 0.5, value)
    if step == 0:
        value = jnp.where(diff >= 0, value, NEG)
    return value


def fill_slab(slab, index, rel_ref, head, top, width, buckets):
    for step in range(top - width + 1, top + 2):
        tile = bias_tile(rel_ref, head, step, buckets)
        for a in range(2):
            p = top + a - step
            if 0 <= p < width:
                slab[index, a * TILE : (a + 1) * TILE, p * TILE : (p + 1) * TILE] = tile


def pair_operands(q, k, v, qm, hot):
    low = lax.broadcasted_iota(jnp.int32, (1, PAIR), 1) < PAIR // 2
    zero = jnp.zeros((), jnp.bfloat16)
    for side in range(2):
        mine = low if side == 0 else jnp.logical_not(low)
        yield (
            jnp.where(mine, q, qm),
            jnp.where(mine, k, hot),
            jnp.where(mine, v, zero),
        )


def first_kernel(
    count, x_ref, x_hbm, w_hbm, rel_ref, len_ref, gate_ref, q_ref, att_ref, recv, head_ref,
    w, normed, k_ref, v_ref, slab, qm_ref, hot_ref, sems, send_sem, recv_sem, head_sem,
):
    rows, width = x_ref.shape
    heads, buckets = rel_ref.shape
    piece = rows // CHUNKS
    me = lax.axis_index("ctx")
    place, plane = lax.rem(me, SPAN), me // SPAN
    planes = count // SPAN
    shift = planes // 4

    def flows(of):
        later = lax.rem(of + shift, planes) + 1
        return jnp.logical_and(later < planes, later != planes // 2)

    sends = flows(plane)
    fed = flows(lax.rem(plane + planes - 1, planes))
    odd = lax.rem(place, 2)
    low = place < 2
    ahead, behind = lax.rem(me + SPAN, count), lax.rem(me + count - SPAN, count)
    after, before = lax.rem(me + 1, count), lax.rem(me + count - 1, count)
    beside = me + 1 - 2 * odd
    opposite = jnp.where(low, me + 2, me - 2)
    relayed = jnp.logical_or(place >= 2, fed)

    barrier = pltpu.get_barrier_semaphore()
    for other in (after, before, beside, opposite):
        pl.semaphore_signal(barrier, inc=1, device_id={"ctx": other}, device_id_type=MESH)

    @pl.when(sends)
    def _():
        pl.semaphore_signal(barrier, inc=1, device_id={"ctx": ahead}, device_id_type=MESH)

    @pl.when(fed)
    def _():
        pl.semaphore_signal(barrier, inc=1, device_id={"ctx": behind}, device_id_type=MESH)

    pl.semaphore_wait(barrier, 4 + sends.astype(jnp.int32) + fed.astype(jnp.int32))

    def part(c):
        return pl.ds(c * piece, piece)

    kinds = {
        0: (sends, None, 3, ahead),
        1: (low, None, 1, opposite),
        2: (odd == 0, None, 0, beside),
        3: (jnp.logical_and(place >= 2, fed), 3, 1, opposite),
        4: (jnp.logical_and(odd == 1, fed), 3, 2, beside),
        5: (jnp.logical_and(relayed, odd == 0), 1, 2, beside),
        6: (jnp.logical_and(relayed, odd == 1), 1, 0, beside),
    }

    def sending(kind, c):
        _, source, slot, to = kinds[kind]
        return pltpu.make_async_remote_copy(
            src_ref=x_hbm.at[part(c)] if source is None else recv.at[source, part(c)],
            dst_ref=recv.at[slot, part(c)],
            send_sem=send_sem.at[kind, c],
            recv_sem=recv_sem.at[slot, c],
            device_id={"ctx": to},
            device_id_type=MESH,
        )

    def start(kind, c):
        @pl.when(kinds[kind][0])
        def _():
            sending(kind, c).start()

    def arrived(slot, c, when):
        @pl.when(when)
        def _():
            pltpu.make_async_copy(
                recv.at[slot, part(c)], recv.at[slot, part(c)], recv_sem.at[slot, c]
            ).wait()

    def earlier(c):
        arrived(3, c, fed)
        start(3, c)
        start(4, c)

    def relay(c):
        arrived(1, c, relayed)
        start(5, c)
        start(6, c)

    for c in range(CHUNKS):
        start(0, c)
        start(1, c)
    for c in range(CHUNKS):
        start(2, c)
    heading = pltpu.make_async_remote_copy(
        src_ref=x_hbm.at[pl.ds(0, 16)],
        dst_ref=head_ref,
        send_sem=head_sem.at[0],
        recv_sem=head_sem.at[1],
        device_id={"ctx": before},
        device_id_type=MESH,
    )
    heading.start()
    order = (1, 3, 2, 0)
    copies = {
        g: pltpu.make_async_copy(
            w_hbm.at[:, g * width : (g + 1) * width], w.at[g], sems.at[g]
        )
        for g in order
    }
    for g in order:
        copies[g].start()
    normed[...] = normalize(x_ref[...].astype(jnp.float32)).astype(jnp.bfloat16)
    qm_ref[...], hot_ref[...] = user_terms(block_time(me, count), rows, ends_of(len_ref))

    def project(g, out, scale):
        def step(j, carry):
            cols = pl.ds(pl.multiple_of(j * 256, 256), 256)
            u = 0.5 * jnp.dot(normed[...], w[g, :, cols], preferred_element_type=jnp.float32)
            y = half_silu(u).astype(jnp.bfloat16)
            out[:, cols] = y if scale is None else y * jnp.asarray(scale, jnp.bfloat16)
            return carry

        copies[g].wait()
        lax.fori_loop(0, width // 256, step, 0)

    project(1, q_ref, 0.5 * (width // heads) ** -0.5)
    project(3, k_ref, None)
    project(2, v_ref, None)
    earlier(0)
    project(0, gate_ref, None)
    earlier(1)

    half = rows // 2

    def pair(hp, carry):
        cols = pl.ds(pl.multiple_of(hp * PAIR, PAIR), PAIR)
        for side in range(2):
            fill_slab(slab, side, rel_ref, 2 * hp + side, 2, 4, buckets)
        tops = []
        for side, (q, k, v) in enumerate(
            pair_operands(q_ref[:, cols], k_ref[:, cols], v_ref[:, cols], qm_ref[...], hot_ref[...])
        ):
            s0 = lax.dot_general(q[:half], k[:half], NT, preferred_element_type=jnp.float32)
            s1 = lax.dot_general(q[half:], k, NT, preferred_element_type=jnp.float32)
            w0 = half_silu(s0 + slab[side, :, half:]).astype(jnp.bfloat16)
            w1 = half_silu(s1 + slab[side]).astype(jnp.bfloat16)
            tops.append(
                (
                    jnp.dot(w0, v[:half], preferred_element_type=jnp.float32),
                    jnp.dot(w1, v, preferred_element_type=jnp.float32),
                )
            )
        att_ref[:half, cols] = tops[0][0] + tops[1][0]
        att_ref[half:, cols] = tops[0][1] + tops[1][1]
        return carry

    lax.fori_loop(0, heads // 4, pair, 0)
    relay(0)
    earlier(2)
    lax.fori_loop(heads // 4, heads // 2, pair, 0)
    relay(1)
    earlier(3)
    relay(2)
    relay(3)
    for c in range(CHUNKS):
        arrived(0, c, jnp.logical_or(odd == 1, relayed))
        arrived(2, c, jnp.logical_or(place == 3, fed))
        for kind in kinds:
            @pl.when(kinds[kind][0])
            def _(kind=kind, c=c):
                sending(kind, c).wait_send()
    heading.wait()


def second_kernel(
    count, list_ref, len_ref, rel_ref, x_ref, gate_ref, q_ref, own_ref, head_ref, cand_ref,
    w_hbm, wout_hbm, recv, out_ref, next_ref, table_ref,
    picked, wkv, wout, normed, kv, att, slab, qm_ref, hot_ref, follow, sems,
):
    rows, width = x_ref.shape
    heads, buckets = rel_ref.shape
    picks = list_ref.shape[1]
    half = rows // 2
    ends = ends_of(len_ref)
    time = block_time(lax.axis_index("ctx"), count)
    useful = []
    for p in range(picks):
        distance = list_ref[0, p]
        last = (time - distance + 1) * rows - 1
        useful.append((distance <= time) & (user_of(last, ends) >= user_of(time * rows, ends)))

        @pl.when(useful[p])
        def _(p=p, distance=distance):
            pltpu.make_async_copy(recv.at[distance - 1], picked.at[p], sems.at[p]).start()
    w_copy = pltpu.make_async_copy(w_hbm.at[:, 2 * width :], wkv, sems.at[picks])
    o_copy = pltpu.make_async_copy(wout_hbm, wout, sems.at[picks + 1])
    w_copy.start()
    o_copy.start()
    att[...] = own_ref[...]
    qm_ref[...] = user_terms(time, rows, ends)[0]
    w_copy.wait()
    for p in range(picks):
        @pl.when(useful[p])
        def _(p=p):
            distance = list_ref[0, p]
            pltpu.make_async_copy(recv.at[0], picked.at[p], sems.at[p]).wait()
            hot_ref[...] = user_terms(time - distance, rows, ends)[1]
            normed[...] = normalize(picked[p].astype(jnp.float32)).astype(jnp.bfloat16)

            def step(j, carry):
                cols = pl.ds(pl.multiple_of(j * 256, 256), 256)
                u = 0.5 * jnp.dot(normed[...], wkv[:, cols], preferred_element_type=jnp.float32)
                kv[:, cols] = half_silu(u).astype(jnp.bfloat16)
                return carry

            lax.fori_loop(0, 2 * width // 256, step, 0)
            for d in range(1, SPAN + 1):
                @pl.when(distance == d)
                def _(d=d):
                    def fill(h, carry):
                        fill_slab(slab, h, rel_ref, h, (rows // TILE) * d + 2, 6, buckets)
                        return carry

                    lax.fori_loop(0, heads, fill, 0)

            def pair(hp, carry):
                cols = pl.ds(pl.multiple_of(hp * PAIR, PAIR), PAIR)
                kcols = pl.ds(pl.multiple_of(width + hp * PAIR, PAIR), PAIR)
                tops = []
                for side, (q, k, v) in enumerate(
                    pair_operands(q_ref[:, cols], kv[:, kcols], kv[:, cols], qm_ref[...], hot_ref[...])
                ):
                    h = 2 * hp + side
                    s0 = lax.dot_general(q[:half], k, NT, preferred_element_type=jnp.float32)
                    s1 = lax.dot_general(q[half:], k, NT, preferred_element_type=jnp.float32)
                    w0 = half_silu(s0 + slab[h, :, half:]).astype(jnp.bfloat16)
                    w1 = half_silu(s1 + slab[h, :, :rows]).astype(jnp.bfloat16)
                    tops.append(
                        (
                            jnp.dot(w0, v, preferred_element_type=jnp.float32),
                            jnp.dot(w1, v, preferred_element_type=jnp.float32),
                        )
                    )
                att[:half, cols] += tops[0][0] + tops[1][0]
                att[half:, cols] += tops[0][1] + tops[1][1]
                return carry

            lax.fori_loop(0, heads // 2, pair, 0)
    o_copy.wait()
    scale = width**-0.5
    last_row = lax.broadcasted_iota(jnp.int32, (rows, 1), 0) == rows - 1
    follow[...] = jnp.where(
        last_row,
        head_ref[0:1, :].astype(jnp.float32),
        pltpu.roll(x_ref[...].astype(jnp.float32), rows - 1, 0),
    )

    def finish(r, carry):
        rs = pl.ds(pl.multiple_of(r * 256, 256), 256)
        gated = (normalize(att[rs, :]) * gate_ref[rs, :].astype(jnp.float32)).astype(jnp.bfloat16)
        added = jnp.dot(gated, wout[...], preferred_element_type=jnp.float32)
        layer = (x_ref[rs, :].astype(jnp.float32) + added).astype(jnp.bfloat16)
        out_ref[rs, :] = layer
        inner = jnp.sum(
            layer.astype(jnp.float32) * follow[rs, :], axis=1, keepdims=True
        )
        at = time * rows + r * 256 + lax.broadcasted_iota(jnp.int32, (256, 1), 0)
        same = (user_of(at + 1, ends) == user_of(at, ends)) & (at + 1 < count * rows)
        next_ref[rs, :] = jnp.where(same, inner * scale, 0.0)
        table_ref[rs, :] = (
            lax.dot_general(layer, cand_ref[...], NT, preferred_element_type=jnp.float32) * scale
        )
        return carry

    lax.fori_loop(0, rows // 256, finish, 0)


def fetch_candidates(events, candidates, ctx_size, my_index):
    event_row_count, hidden_width = events.shape
    cand_count = candidates.shape[1]
    slot_cap = 2 * cand_count // ctx_size
    number = jnp.arange(cand_count, dtype=jnp.int32)
    before = number[:, None] < number[None, :]
    mine = candidates // event_row_count == my_index
    rank = jnp.dot(
        mine.astype(jnp.bfloat16), before.astype(jnp.bfloat16), preferred_element_type=jnp.float32
    ).astype(jnp.int32)
    local = jnp.where(mine, candidates % event_row_count, -1)
    slots = jnp.arange(slot_cap, dtype=jnp.int32)
    ids = jnp.max(
        jnp.where(rank[:, None, :] == slots[None, :, None], local[:, None, :], -1), axis=2
    ).reshape(-1)
    picks = (ids[:, None] == jnp.arange(event_row_count, dtype=jnp.int32)[None, :]).astype(jnp.bfloat16)
    fetched = jnp.dot(picks, events, preferred_element_type=jnp.float32).astype(jnp.bfloat16)
    arrived_rows = lax.all_to_all(
        fetched.reshape(ctx_size, slot_cap, hidden_width), "ctx", split_axis=0, concat_axis=0, tiled=True
    )
    owner = lax.dynamic_slice_in_dim(candidates, my_index, 1, 0)[0] // event_row_count
    own_rank = jnp.sum(
        ((owner[:, None] == owner[None, :]) & before.T).astype(jnp.int32), axis=1
    )
    own_slot = owner * slot_cap + own_rank
    own_hits = own_slot[:, None] == jnp.arange(ctx_size * slot_cap, dtype=jnp.int32)[None, :]
    return jnp.dot(
        own_hits.astype(jnp.bfloat16),
        arrived_rows.reshape(ctx_size * slot_cap, hidden_width),
        preferred_element_type=jnp.float32,
    ).astype(jnp.bfloat16)


def shards(events, w_in, w_out, rel_bias, lengths, block_lists, candidates):
    rows, width = events.shape
    heads = rel_bias.shape[0]
    picks = block_lists.shape[1]
    count = lax.axis_size("ctx")
    cand = fetch_candidates(events, candidates, count, lax.axis_index("ctx"))

    vm = pl.BlockSpec(memory_space=pltpu.VMEM)
    sm = pl.BlockSpec(memory_space=pltpu.SMEM)
    hb = pl.BlockSpec(memory_space=pl.ANY)
    bf, f32 = jnp.bfloat16, jnp.float32
    gate, q, own, recv, following = pl.pallas_call(
        functools.partial(first_kernel, count),
        out_shape=(
            jax.ShapeDtypeStruct((rows, width), bf),
            jax.ShapeDtypeStruct((rows, width), bf),
            jax.ShapeDtypeStruct((rows, width), f32),
            jax.ShapeDtypeStruct((SPAN, rows, width), bf),
            jax.ShapeDtypeStruct((16, width), bf),
        ),
        in_specs=[vm, hb, hb, sm, sm],
        out_specs=(vm, vm, vm, hb, hb),
        scratch_shapes=[
            pltpu.VMEM((4, width, width), bf),
            pltpu.VMEM((rows, width), bf),
            pltpu.VMEM((rows, width), bf),
            pltpu.VMEM((rows, width), bf),
            pltpu.VMEM((2, 2 * TILE, 4 * TILE), f32),
            pltpu.VMEM((rows, PAIR), bf),
            pltpu.VMEM((rows, PAIR), bf),
            pltpu.SemaphoreType.DMA((4,)),
            pltpu.SemaphoreType.DMA((7, CHUNKS)),
            pltpu.SemaphoreType.DMA((SPAN, CHUNKS)),
            pltpu.SemaphoreType.DMA((2,)),
        ],
        compiler_params=pltpu.CompilerParams(
            vmem_limit_bytes=VMEM_LIMIT, collective_id=0, has_side_effects=True
        ),
        cost_estimate=pl.CostEstimate(
            flops=2 * rows * width * 4 * width + 4 * rows * rows * width,
            bytes_accessed=10 * width * width,
            transcendentals=heads * rows * rows,
        ),
        name="project_and_own_block",
    )(events, events, w_in, rel_bias, lengths)
    layer_output, next_score, scores = pl.pallas_call(
        functools.partial(second_kernel, count),
        out_shape=(
            jax.ShapeDtypeStruct((rows, width), bf),
            jax.ShapeDtypeStruct((rows, 1), f32),
            jax.ShapeDtypeStruct((rows, candidates.shape[1]), f32),
        ),
        in_specs=[sm, sm, sm, vm, vm, vm, vm, vm, vm, hb, hb, hb],
        out_specs=(vm, vm, vm),
        scratch_shapes=[
            pltpu.VMEM((picks, rows, width), bf),
            pltpu.VMEM((width, 2 * width), bf),
            pltpu.VMEM((width, width), bf),
            pltpu.VMEM((rows, width), bf),
            pltpu.VMEM((rows, 2 * width), bf),
            pltpu.VMEM((rows, width), f32),
            pltpu.VMEM((heads, 2 * TILE, 6 * TILE), f32),
            pltpu.VMEM((rows, PAIR), bf),
            pltpu.VMEM((rows, PAIR), bf),
            pltpu.VMEM((rows, width), f32),
            pltpu.SemaphoreType.DMA((picks + 2,)),
        ],
        compiler_params=pltpu.CompilerParams(vmem_limit_bytes=VMEM_LIMIT),
        cost_estimate=pl.CostEstimate(
            flops=2 * picks * (2 * rows * width * width + 2 * rows * rows * width),
            bytes_accessed=16 * width * width,
            transcendentals=2 * heads * rows * rows,
        ),
        name="earlier_blocks_and_output",
    )(
        block_lists, lengths, rel_bias, events, gate, q, own, following, cand, w_in, w_out, recv,
    )
    return (layer_output, next_score[:, 0], scores)


def solution(mesh):
    in_specs = (
        P(("groups", "ctx"), None),
        P(),
        P(),
        P(),
        P("groups"),
        P(("groups", "ctx"), None),
        P("groups", None),
    )
    out_specs = (P(("groups", "ctx"), None), P(("groups", "ctx")), P(("groups", "ctx"), None))
    return jax.shard_map(shards, mesh=mesh, in_specs=in_specs, out_specs=out_specs, check_vma=False)
```

time: 125 us -> 96.4 us (0.77)
  Pallas kernels: 50.6 us -> 78.4 us
  waiting for transfers between devices: 16.1 us -> 0.01 us
  starting transfers between devices: 21.9 us -> 7.38 us
  other arithmetic: 16.4 us -> 5.02 us
  between operations: 10 us -> 0.68 us
  local copies, waits for them, and re-layouts: 6.07 us -> 0.08 us
    pallas_call x2, Pallas kernels: 50.6 us -> 78.4 us  [the longest x1 45.7 us: shards(): pl.pallas_call(functools.partial(first_kernel, count), out_shape=(jax.Sha...]
    ppermute x8 -> x0, starting transfers between devices: 17.1 us -> none  [the longest x1 5.07 us: received(): a2 = lax.ppermute(events, 'ctx', inside(((0, 2), (1, 3))))]
    ppermute x8 -> x0, waiting for transfers between devices: 16.1 us -> none  [the longest x1 15.2 us: received(): b3 = lax.ppermute(b1, 'ctx', inside(((2, 0), (3, 1)), fed))]
    another operation x7 -> x0, other arithmetic: 7.08 us -> none  [the longest x3 3.17 us: shards(): info = jnp.stack(infos)]
    slice x9 -> x0, local copies, waits for them, and re-layouts: 5.04 us -> none  [the longest x6 3.44 us: shards(): useful = (key_pos[0] < query_pos[0]) & (key_user[rows - 1] >= query_user[0])]
    all_to_all x1, starting transfers between devices: 4.72 us -> 7.38 us  [fetch_candidates(): lax.all_to_all(fetched.reshape(ctx_size, slot_cap, hidden_width), 'ctx',...]
    convert_element_type x4 -> x0, other arithmetic: 2.55 us -> none  [the longest x1 0.88 us: shards(): next_ok.astype(f32)[:, None]]
  transfers between devices with their start and end apart: 9 -> 1, of which waited for: 2 -> 0; matrix products, arithmetic and copies ran while one was open for 19% -> 2% of each run, Pallas kernels for 14% -> 48%
where the time goes in v1:
time: 96.4 us; the launch traced here: 95.9 us
  Pallas kernels  78.4 us (81%)
  starting transfers between devices  7.38 us (8%)
  other arithmetic  5.02 us (5%)
  matrix products  4.33 us (4%)
    pallas_call x1, Pallas kernels, shards(): pl.pallas_call(functools.partial(first_kernel, count), out_shape=(jax.Sha...  45.7 us
    pallas_call x1, Pallas kernels, shards(): pl.pallas_call(functools.partial(second_kernel, count), out_shape=(jax.Sh...  32.8 us
    all_to_all x1, starting transfers between devices, fetch_candidates(): lax.all_to_all(fetched.reshape(ctx_size, slot_cap, hidden_width), 'ctx',...  7.38 us
    dot_general x1, matrix products, fetch_candidates(): jnp.dot(picks, events, preferred_element_type=jnp.float32)  2.51 us
  transfers between devices with their start and end apart: 1, of which 0 were waited for; matrix products, arithmetic and copies ran while one was open for 2% of the time, Pallas kernels for 48%

profile of v1, /device:TPU:0, one launch (start us, length us, event | category | flops | bytes accessed | tf_op | source)
XLA Modules:
  0.0 95.9 jit_solution(10840579343622243367)
XLA Ops:
  0.6 0.7 fusion.4
  1.3 0.8 convolution_convert_fusion.2
  2.2 0.3 select_reduce_fusion
  2.5 0.1 eq.76
  2.6 2.5 %convolution_convert_fusion = bf16[256,1024]{1,0:T(8,128)(2,1)} fusion(bf16[512,1024]{1,0:T(8,128)(2,1)} %x_ref.3, s32[256]{0:T(256)S(1)} %eq.76), kind=kOutput, calls=%fused_computation | convolution fusion | flops 268828672 | bytes 1573888 | tf_op jit(solution)/shard_map/dot_general | solution.py:391
  5.1 7.4 %all-to-all-start = ((bf16[16,16,1024]{2,1,0:T(8,128)(2,1)}), bf16[16,16,1024]{2,1,0:T(8,128)(2,1)S(1)}, u32[]{:S(2)}, u32[]{:S(2)}) async-start(bf16[16,16,1024]{2,1,0:T(8,128)(2,1)} %bitcast.2), calls=%async_computation | async-start | bytes 1048576 | tf_op jit(solution)/shard_map/all_to_all | solution.py:392
  12.5 0.7 fusion.7
  13.2 0.7 and_select_fusion.1
  13.9 0.2 convert_reduce_fusion
  14.1 0.7 multiply_add_fusion
  14.8 45.7 %project_and_own_block.1 = (bf16[512,1024]{1,0:T(8,128)(2,1)}, bf16[512,1024]{1,0:T(8,128)(2,1)}, f32[512,1024]{1,0:T(8,128)}, bf16[4,512,1024]{2,1,0:T(8,128)(2,1)}, bf16[16,1024]{1,0:T(8,128)(2,1)}) custom-call(bf16[512,1024]{1,0:T(8,128)(2,1)} %x_ref.3, bf16[512,1024]{1,0:T(8,128)(2,1)} %x_ref.3, bf16[1024,4096]{1,0:T(8,128)(2,1)} %w_hbm.3, ...), custom_call_target="tpu_custom_call" | custom-call | flops 5368709120 | bytes 10485760 | tf_op jit(solution)/shard_map/project_and_own_block/pallas_call | solution.py:419
  60.5 0.0 all-to-all-done
  60.5 1.0 %convolution_convert_fusion.1.cand_ref = bf16[128,1024]{1,0:T(8,128)(2,1)} fusion(bf16[256,1024]{1,0:T(8,128)(2,1)S(1)} %bitcast.16, s32[128]{0:T(128)S(1)} %multiply_add_fusion), kind=kOutput, calls=%fused_computation.1 | convolution fusion | flops 67272704 | bytes 786944 | tf_op jit(solution)/shard_map/dot_general | solution.py:401
  61.5 32.8 %earlier_blocks_and_output.1 = (bf16[512,1024]{1,0:T(8,128)(2,1)}, f32[512,1]{1,0:T(8,128)}, f32[512,128]{1,0:T(8,128)}) custom-call(s32[1,2]{1,0:T(1,128)} %list_ref.1, s32[4]{0:T(128)} %len_ref.3, f32[16,16]{1,0:T(8,128)} %rel_ref.3, bf16[512,1024]{1,0:T(8,128)(2,1)} %x_ref.3, bf16[512,1024]{1,0:T(8,128)(2,1)} %get-tuple-element.11.gate_ref, ...), custom_call_target="tpu_custom_call" | custom-call | flops 6442450944 | bytes 16777216 | tf_op jit(solution)/shard_map/earlier_blocks_and_output/pallas_call | solution.py:453
  94.2 1.7 %reduce = f32[512]{0:T(512)} reduce(f32[512,1]{1,0:T(8,128)} %get-tuple-element.17, f32[]{:T(128)} %constant.49), dimensions={1}, to_apply=%get-tuple-element.17.reduce_sub_computation | reduce | bytes 4100 | tf_op jit(solution)/shard_map/earlier_blocks_and_output/pallas_call | solution.py:453
Async XLA Ops:
  5.1 55.4 %all-to-all-start = ((bf16[16,16,1024]{2,1,0:T(8,128)(2,1)}), bf16[16,16,1024]{2,1,0:T(8,128)(2,1)S(1)}, u32[]{:S(2)}, u32[]{:S(2)}) async-start(bf16[16,16,1024]{2,1,0:T(8,128)(2,1)} %bitcast.2), calls=%async_computation | async-start | bytes 1048576 | tf_op jit(solution)/shard_map/all_to_all | solution.py:392

commit v2 on v1

--- a/solution.py
+++ b/solution.py
@@ -12,7 +12,7 @@
 TILE = 128
 PAIR = 128
 VMEM_LIMIT = 56 * 1024 * 1024
-CHUNKS = 4
+CHUNKS = 8
 MESH = pl.DeviceIdType.MESH
 
 NT = (((1,), (1,)), ((), ()))
@@ -98,8 +98,8 @@
 
 
 def first_kernel(
-    count, x_ref, x_hbm, w_hbm, rel_ref, len_ref, gate_ref, q_ref, att_ref, recv, head_ref,
-    w, normed, k_ref, v_ref, slab, qm_ref, hot_ref, sems, send_sem, recv_sem, head_sem,
+    count, x_ref, x_hbm, w_hbm, rel_ref, len_ref, picks_ref, gate_ref, q_ref, att_ref, recv, head_ref, cand_recv,
+    w, normed, k_ref, v_ref, slab, qm_ref, hot_ref, fetched, sems, send_sem, recv_sem, head_sem, cand_send, cand_sem,
 ):
     rows, width = x_ref.shape
     heads, buckets = rel_ref.shape
@@ -117,25 +117,21 @@
     fed = flows(lax.rem(plane + planes - 1, planes))
     odd = lax.rem(place, 2)
     low = place < 2
-    ahead, behind = lax.rem(me + SPAN, count), lax.rem(me + count - SPAN, count)
-    after, before = lax.rem(me + 1, count), lax.rem(me + count - 1, count)
+    ahead = lax.rem(me + SPAN, count)
+    before = lax.rem(me + count - 1, count)
     beside = me + 1 - 2 * odd
     opposite = jnp.where(low, me + 2, me - 2)
     relayed = jnp.logical_or(place >= 2, fed)
 
     barrier = pltpu.get_barrier_semaphore()
-    for other in (after, before, beside, opposite):
+
+    def greet(j, carry):
+        other = lax.rem(me + j, count)
         pl.semaphore_signal(barrier, inc=1, device_id={"ctx": other}, device_id_type=MESH)
-
-    @pl.when(sends)
-    def _():
-        pl.semaphore_signal(barrier, inc=1, device_id={"ctx": ahead}, device_id_type=MESH)
-
-    @pl.when(fed)
-    def _():
-        pl.semaphore_signal(barrier, inc=1, device_id={"ctx": behind}, device_id_type=MESH)
-
-    pl.semaphore_wait(barrier, 4 + sends.astype(jnp.int32) + fed.astype(jnp.int32))
+        return carry
+
+    lax.fori_loop(1, count, greet, 0)
+    pl.semaphore_wait(barrier, count - 1)
 
     def part(c):
         return pl.ds(c * piece, piece)
@@ -197,6 +193,31 @@
         device_id_type=MESH,
     )
     heading.start()
+    cap = picks_ref.shape[0] // count
+    fetched[...] = (
+        jnp.dot(picks_ref[...], x_ref[...], preferred_element_type=jnp.float32)
+        .astype(jnp.bfloat16)
+        .reshape(count, cap, width)
+    )
+
+    def candidate(j):
+        to = lax.rem(me + j, count)
+        return pltpu.make_async_remote_copy(
+            src_ref=fetched.at[to],
+            dst_ref=cand_recv.at[me],
+            send_sem=cand_send.at[j],
+            recv_sem=cand_sem.at[me],
+            device_id={"ctx": to},
+            device_id_type=MESH,
+        )
+
+    def send_candidate(j, carry):
+        candidate(j).start()
+        return carry
+
+    lax.fori_loop(1, count, send_candidate, 0)
+    own_rows = pltpu.make_async_copy(fetched.at[me], cand_recv.at[me], cand_send.at[0])
+    own_rows.start()
     order = (1, 3, 2, 0)
     copies = {
         g: pltpu.make_async_copy(
@@ -251,14 +272,30 @@
         att_ref[half:, cols] = tops[0][1] + tops[1][1]
         return carry
 
-    lax.fori_loop(0, heads // 4, pair, 0)
+    pairs = heads // 2
+    lax.fori_loop(0, pairs // 4, pair, 0)
+    earlier(2)
     relay(0)
-    earlier(2)
-    lax.fori_loop(heads // 4, heads // 2, pair, 0)
+    lax.fori_loop(pairs // 4, pairs * 5 // 8, pair, 0)
+    earlier(3)
     relay(1)
-    earlier(3)
-    relay(2)
-    relay(3)
+    lax.fori_loop(pairs * 5 // 8, pairs, pair, 0)
+    for c in range(4, CHUNKS):
+        earlier(c)
+        relay(c - 2)
+    relay(CHUNKS - 2)
+    relay(CHUNKS - 1)
+
+    def end_candidate(j, carry):
+        source = lax.rem(me + j, count)
+        pltpu.make_async_copy(
+            cand_recv.at[source], cand_recv.at[source], cand_sem.at[source]
+        ).wait()
+        candidate(j).wait_send()
+        return carry
+
+    own_rows.wait()
+    lax.fori_loop(1, count, end_candidate, 0)
     for c in range(CHUNKS):
         arrived(0, c, jnp.logical_or(odd == 1, relayed))
         arrived(2, c, jnp.logical_or(place == 3, fed))
@@ -363,7 +400,13 @@
         )
         at = time * rows + r * 256 + lax.broadcasted_iota(jnp.int32, (256, 1), 0)
         same = (user_of(at + 1, ends) == user_of(at, ends)) & (at + 1 < count * rows)
-        next_ref[rs, :] = jnp.where(same, inner * scale, 0.0)
+        score = jnp.where(same, inner * scale, 0.0)
+        eye = lax.broadcasted_iota(jnp.int32, (TILE, TILE), 0) == lax.broadcasted_iota(
+            jnp.int32, (TILE, TILE), 1
+        )
+        for j in range(256 // TILE):
+            spread = jnp.where(eye, score[j * TILE : (j + 1) * TILE], 0.0)
+            next_ref[r * (256 // TILE) + j] = jnp.sum(spread, axis=0, keepdims=True)
         table_ref[rs, :] = (
             lax.dot_general(layer, cand_ref[...], NT, preferred_element_type=jnp.float32) * scale
         )
@@ -372,10 +415,9 @@
     lax.fori_loop(0, rows // 256, finish, 0)
 
 
-def fetch_candidates(events, candidates, ctx_size, my_index):
-    event_row_count, hidden_width = events.shape
+def candidate_slots(candidates, event_row_count, ctx_size, my_index):
     cand_count = candidates.shape[1]
-    slot_cap = 2 * cand_count // ctx_size
+    slot_cap = max(2 * cand_count // ctx_size, 16)
     number = jnp.arange(cand_count, dtype=jnp.int32)
     before = number[:, None] < number[None, :]
     mine = candidates // event_row_count == my_index
@@ -388,21 +430,13 @@
         jnp.where(rank[:, None, :] == slots[None, :, None], local[:, None, :], -1), axis=2
     ).reshape(-1)
     picks = (ids[:, None] == jnp.arange(event_row_count, dtype=jnp.int32)[None, :]).astype(jnp.bfloat16)
-    fetched = jnp.dot(picks, events, preferred_element_type=jnp.float32).astype(jnp.bfloat16)
-    arrived_rows = lax.all_to_all(
-        fetched.reshape(ctx_size, slot_cap, hidden_width), "ctx", split_axis=0, concat_axis=0, tiled=True
-    )
     owner = lax.dynamic_slice_in_dim(candidates, my_index, 1, 0)[0] // event_row_count
     own_rank = jnp.sum(
         ((owner[:, None] == owner[None, :]) & before.T).astype(jnp.int32), axis=1
     )
     own_slot = owner * slot_cap + own_rank
     own_hits = own_slot[:, None] == jnp.arange(ctx_size * slot_cap, dtype=jnp.int32)[None, :]
-    return jnp.dot(
-        own_hits.astype(jnp.bfloat16),
-        arrived_rows.reshape(ctx_size * slot_cap, hidden_width),
-        preferred_element_type=jnp.float32,
-    ).astype(jnp.bfloat16)
+    return picks, own_hits.astype(jnp.bfloat16)
 
 
 def shards(events, w_in, w_out, rel_bias, lengths, block_lists, candidates):
@@ -410,13 +444,14 @@
     heads = rel_bias.shape[0]
     picks = block_lists.shape[1]
     count = lax.axis_size("ctx")
-    cand = fetch_candidates(events, candidates, count, lax.axis_index("ctx"))
+    asked, own_hits = candidate_slots(candidates, rows, count, lax.axis_index("ctx"))
+    cap = asked.shape[0] // count
 
     vm = pl.BlockSpec(memory_space=pltpu.VMEM)
     sm = pl.BlockSpec(memory_space=pltpu.SMEM)
     hb = pl.BlockSpec(memory_space=pl.ANY)
     bf, f32 = jnp.bfloat16, jnp.float32
-    gate, q, own, recv, following = pl.pallas_call(
+    gate, q, own, recv, following, arrived_rows = pl.pallas_call(
         functools.partial(first_kernel, count),
         out_shape=(
             jax.ShapeDtypeStruct((rows, width), bf),
@@ -424,9 +459,10 @@
             jax.ShapeDtypeStruct((rows, width), f32),
             jax.ShapeDtypeStruct((SPAN, rows, width), bf),
             jax.ShapeDtypeStruct((16, width), bf),
+            jax.ShapeDtypeStruct((count, cap, width), bf),
         ),
-        in_specs=[vm, hb, hb, sm, sm],
-        out_specs=(vm, vm, vm, hb, hb),
+        in_specs=[vm, hb, hb, sm, sm, vm],
+        out_specs=(vm, vm, vm, hb, hb, hb),
         scratch_shapes=[
             pltpu.VMEM((4, width, width), bf),
             pltpu.VMEM((rows, width), bf),
@@ -435,10 +471,13 @@
             pltpu.VMEM((2, 2 * TILE, 4 * TILE), f32),
             pltpu.VMEM((rows, PAIR), bf),
             pltpu.VMEM((rows, PAIR), bf),
+            pltpu.VMEM((count, cap, width), bf),
             pltpu.SemaphoreType.DMA((4,)),
             pltpu.SemaphoreType.DMA((7, CHUNKS)),
             pltpu.SemaphoreType.DMA((SPAN, CHUNKS)),
             pltpu.SemaphoreType.DMA((2,)),
+            pltpu.SemaphoreType.DMA((count,)),
+            pltpu.SemaphoreType.DMA((count,)),
         ],
         compiler_params=pltpu.CompilerParams(
             vmem_limit_bytes=VMEM_LIMIT, collective_id=0, has_side_effects=True
@@ -449,12 +488,15 @@
             transcendentals=heads * rows * rows,
         ),
         name="project_and_own_block",
-    )(events, events, w_in, rel_bias, lengths)
+    )(events, events, w_in, rel_bias, lengths, asked)
+    cand = jnp.dot(
+        own_hits, arrived_rows.reshape(count * cap, width), preferred_element_type=f32
+    ).astype(bf)
     layer_output, next_score, scores = pl.pallas_call(
         functools.partial(second_kernel, count),
         out_shape=(
             jax.ShapeDtypeStruct((rows, width), bf),
-            jax.ShapeDtypeStruct((rows, 1), f32),
+            jax.ShapeDtypeStruct((rows // TILE, 1, TILE), f32),
             jax.ShapeDtypeStruct((rows, candidates.shape[1]), f32),
         ),
         in_specs=[sm, sm, sm, vm, vm, vm, vm, vm, vm, hb, hb, hb],
@@ -482,7 +524,7 @@
     )(
         block_lists, lengths, rel_bias, events, gate, q, own, following, cand, w_in, w_out, recv,
     )
-    return (layer_output, next_score[:, 0], scores)
+    return (layer_output, next_score.reshape(rows), scores)
 
 
 def solution(mesh):

time: 96.4 us -> 88.9 us (0.922)
  starting transfers between devices: 7.38 us -> 0 us
  Pallas kernels: 78.4 us -> 80.8 us
  matrix products: 4.33 us -> 2.87 us
    all_to_all x1 -> x0, starting transfers between devices: 7.38 us -> none  [fetch_candidates(): lax.all_to_all(fetched.reshape(ctx_size, slot_cap, hidden_width), 'ctx',...]
    pallas_call x1, Pallas kernels: 45.7 us -> 48.1 us  [shards(): pl.pallas_call(functools.partial(first_kernel, count), out_shape=(jax.Sha...]
    pallas_call x1 -> x0, other arithmetic: 1.68 us -> none  [shards(): pl.pallas_call(functools.partial(second_kernel, count), out_shape=(jax.Sh...]
    dot_general x3 -> x2, matrix products: 4.33 us -> 2.87 us  [the longest x1 2.04 us: shards(): jnp.dot(own_hits, arrived_rows.reshape(count * cap, width), preferred_ele...]
  transfers between devices with their start and end apart: 1 -> 0, of which waited for: 0 -> 0; matrix products, arithmetic and copies ran while one was open for 2% -> 0% of each run, Pallas kernels for 48% -> 0%
where the time goes in v2:
time: 88.9 us; the launch traced here: 88.5 us
  Pallas kernels  80.8 us (91%)
  other arithmetic  4.16 us (5%)
  matrix products  2.87 us (3%)
    pallas_call x1, Pallas kernels, shards(): pl.pallas_call(functools.partial(first_kernel, count), out_shape=(jax.Sha...  48.1 us
    pallas_call x1, Pallas kernels, shards(): pl.pallas_call(functools.partial(second_kernel, count), out_shape=(jax.Sh...  32.7 us
    dot_general x1, matrix products, shards(): jnp.dot(own_hits, arrived_rows.reshape(count * cap, width), preferred_ele...  2.04 us

profile of v2, /device:TPU:0, one launch (start us, length us, event | category | flops | bytes accessed | tf_op | source)
XLA Modules:
  0.0 88.5 jit_solution(3381802827471743473)
XLA Ops:
  0.6 0.7 fusion.7
  1.3 0.7 and_select_fusion.1
  2.0 0.2 convert_reduce_fusion
  2.2 0.7 multiply_add_fusion
  2.9 0.8 convolution_convert_fusion.1
  3.8 0.7 fusion.4
  4.5 0.3 select_reduce_fusion
  4.8 0.1 eq.69
  4.9 0.8 fusion.picks_ref
  5.7 48.1 %project_and_own_block.1 = (bf16[512,1024]{1,0:T(8,128)(2,1)}, bf16[512,1024]{1,0:T(8,128)(2,1)}, f32[512,1024]{1,0:T(8,128)}, bf16[4,512,1024]{2,1,0:T(8,128)(2...) custom-call(bf16[512,1024]{1,0:T(8,128)(2,1)} %x_ref.3, bf16[512,1024]{1,0:T(8,128)(2,1)} %x_ref.3, ...), custom_call_target="tpu_custom_call" | custom-call | flops 5368709120 | bytes 10485760 | tf_op jit(solution)/shard_map/project_and_own_block/pallas_call | solution.py:454
  53.8 2.0 %convolution_convert_fusion.cand_ref = bf16[128,1024]{1,0:T(8,128)(2,1)} fusion(bf16[256,1024]{1,0:T(8,128)(2,1)} %bitcast.15, s32[128]{0:T(128)S(1)} %multiply_add_fusion), kind=kOutput, calls=%fused_computation | convolution fusion | flops 67272704 | bytes 786944 | tf_op jit(solution)/shard_map/dot_general | solution.py:492
  55.8 32.7 %earlier_blocks_and_output.1 = (bf16[512,1024]{1,0:T(8,128)(2,1)}, f32[4,1,128]{2,1,0:T(1,128)}, f32[512,128]{1,0:T(8,128)}) custom-call(s32[1,2]{1,0:T(1,128)} %list_ref.1, s32[4]{0:T(128)} %len_ref.3, f32[16,16]{1,0:T(8,128)} %rel_ref.3, bf16[512,1024]{1,0:T(8,128)(2,1)} %x_ref.3, bf16[512,1024]{1,0:T(8,128)(2,1)} %get-tuple-element.12.gate_ref, ...), custom_call_target="tpu_custom_call" | custom-call | flops 6442450944 | bytes 16777216 | tf_op jit(solution)/shard_map/earlier_blocks_and_output/pallas_call | solution.py:495

commit v3 on v2

--- a/solution.py
+++ b/solution.py
@@ -347,7 +347,7 @@
                 kv[:, cols] = half_silu(u).astype(jnp.bfloat16)
                 return carry
 
-            lax.fori_loop(0, 2 * width // 256, step, 0)
+            lax.fori_loop(0, 2 * width // 256, step, 0, unroll=2)
             for d in range(1, SPAN + 1):
                 @pl.when(distance == d)
                 def _(d=d):
@@ -379,7 +379,7 @@
                 att[half:, cols] += tops[0][1] + tops[1][1]
                 return carry
 
-            lax.fori_loop(0, heads // 2, pair, 0)
+            lax.fori_loop(0, heads // 2, pair, 0, unroll=2)
     o_copy.wait()
     scale = width**-0.5
     last_row = lax.broadcasted_iota(jnp.int32, (rows, 1), 0) == rows - 1
@@ -412,7 +412,7 @@
         )
         return carry
 
-    lax.fori_loop(0, rows // 256, finish, 0)
+    lax.fori_loop(0, rows // 256, finish, 0, unroll=2)
 
 
 def candidate_slots(candidates, event_row_count, ctx_size, my_index):

time: 88.9 us -> 86.4 us (0.972)
  Pallas kernels: 80.8 us -> 78.2 us
    pallas_call x1, Pallas kernels: 32.7 us -> 30.2 us  [shards(): pl.pallas_call(functools.partial(second_kernel, count), out_shape=(jax.Sh...]
where the time goes in v3:
time: 86.4 us; the launch traced here: 86 us
  Pallas kernels  78.2 us (91%)
  other arithmetic  4.16 us (5%)
  matrix products  2.87 us (3%)
    pallas_call x1, Pallas kernels, shards(): pl.pallas_call(functools.partial(first_kernel, count), out_shape=(jax.Sha...  48.1 us
    pallas_call x1, Pallas kernels, shards(): pl.pallas_call(functools.partial(second_kernel, count), out_shape=(jax.Sh...  30.2 us
    dot_general x1, matrix products, shards(): jnp.dot(own_hits, arrived_rows.reshape(count * cap, width), preferred_ele...  2.04 us

profile of v3, /device:TPU:0, one launch (start us, length us, event | category | flops | bytes accessed | tf_op | source)
XLA Modules:
  0.0 86.0 jit_solution(9917345117134312247)
XLA Ops:
  0.6 0.7 fusion.7
  1.3 0.7 and_select_fusion.1
  2.0 0.2 convert_reduce_fusion
  2.2 0.7 multiply_add_fusion
  2.9 0.8 convolution_convert_fusion.1
  3.8 0.7 fusion.4
  4.5 0.3 select_reduce_fusion
  4.8 0.1 eq.69
  4.9 0.8 fusion.picks_ref
  5.7 48.1 %project_and_own_block.1 = (bf16[512,1024]{1,0:T(8,128)(2,1)}, bf16[512,1024]{1,0:T(8,128)(2,1)}, f32[512,1024]{1,0:T(8,128)}, bf16[4,512,1024]{2,1,0:T(8,128)(2...) custom-call(bf16[512,1024]{1,0:T(8,128)(2,1)} %x_ref.3, bf16[512,1024]{1,0:T(8,128)(2,1)} %x_ref.3, ...), custom_call_target="tpu_custom_call" | custom-call | flops 5368709120 | bytes 10485760 | tf_op jit(solution)/shard_map/project_and_own_block/pallas_call | solution.py:454
  53.8 2.0 %convolution_convert_fusion.cand_ref = bf16[128,1024]{1,0:T(8,128)(2,1)} fusion(bf16[256,1024]{1,0:T(8,128)(2,1)} %bitcast.15, s32[128]{0:T(128)S(1)} %multiply_add_fusion), kind=kOutput, calls=%fused_computation | convolution fusion | flops 67272704 | bytes 786944 | tf_op jit(solution)/shard_map/dot_general | solution.py:492
  55.8 30.2 %earlier_blocks_and_output.1 = (bf16[512,1024]{1,0:T(8,128)(2,1)}, f32[4,1,128]{2,1,0:T(1,128)}, f32[512,128]{1,0:T(8,128)}) custom-call(s32[1,2]{1,0:T(1,128)} %list_ref.1, s32[4]{0:T(128)} %len_ref.3, f32[16,16]{1,0:T(8,128)} %rel_ref.3, bf16[512,1024]{1,0:T(8,128)(2,1)} %x_ref.3, bf16[512,1024]{1,0:T(8,128)(2,1)} %get-tuple-element.12.gate_ref, ...), custom_call_target="tpu_custom_call" | custom-call | flops 6442450944 | bytes 16777216 | tf_op jit(solution)/shard_map/earlier_blocks_and_output/pallas_call | solution.py:495
